TPU v7x, 32 devices: a whole 2x2x4 slice. The times are simulated.
32 devices in a mesh: grid: 4 (over y, x), dom: 8 (over z, core).
Axes of the slice: x: 2, y: 2, z: 4, core: 2. Of those that a mesh axis runs over, the one named last changes fastest.
Arguments:
- state_field: float32 [4, 16, 8, 16384], P('grid', 'dom'), may hold values from -6 to 6
- level_vectors: int32 [4, 4], P('grid'), may hold values from 2 to 5, as said below
- combine_weights: int32 [4], P('grid'), may hold values from -2 to 2, as said below
- diffusion: float32 [6], replicated, may hold values from 0.05 to 0.08
- courant: float32 [6], replicated, may hold values from -0.3 to 0.3
Outputs:
- combined_field: float32 [4, 16, 8, 16384], P('grid', 'dom')
Inputs may be any that keep to these rules, and one draw needn't show every extreme that they name: `level_vectors`: each row holds 2, 3, 4, 5 in some order. `combine_weights`: never zero.
All inputs are finite; a program needn't handle non-finite values.
Results may differ from a plain program's by a relative error of at most 0.0003.
Values sent between devices are 32-bit elements; how exact they have to be, the bound alone decides.
A program may use at most 128 MiB of HBM per device.

v0:
```python
import jax
import jax.numpy as jnp
from jax import lax
from jax.sharding import PartitionSpec as P

LOW = 2


def with_halo(x, sides, width):
    for axis, dim in sides:
        peers, length = (lax.axis_size(axis), x.shape[dim])
        up = [(i, (i + 1) % peers) for i in range(peers)]
        down = [(j, i) for i, j in up]
        last = lax.slice_in_dim(x, length - width, length, axis=dim)
        initial = lax.slice_in_dim(x, 0, width, axis=dim)
        before = lax.ppermute(last, axis, up)
        after = lax.ppermute(initial, axis, down)
        x = jnp.concatenate([before, x, after], axis=dim)
    return x


def spacings(length, orientation):
    ladder = [2**exponent for exponent in range(length.bit_length() - 1)]
    return ladder if orientation < 0 else ladder[::-1]


def digit_table(count, stride, length):
    return jnp.arange(count, dtype=jnp.int32) // stride % length


def flat_forward(values, stride, length, distance):
    digit = digit_table(values.shape[-1], stride, length)
    wrapped = jnp.roll(values, (length - distance) * stride, -1)
    plain = jnp.roll(values, -distance * stride, -1)
    return jnp.where(digit >= length - distance, wrapped, plain)


def flat_backward(values, stride, length, distance):
    digit = digit_table(values.shape[-1], stride, length)
    wrapped = jnp.roll(values, -(length - distance) * stride, -1)
    plain = jnp.roll(values, distance * stride, -1)
    return jnp.where(digit < distance, wrapped, plain)


def flat_level(values, stride, length, spacing, orientation):
    digit = digit_table(values.shape[-1], stride, length)
    lower = flat_backward(values, stride, length, spacing)
    upper = flat_forward(values, stride, length, spacing)
    active = digit % (2 * spacing) == spacing
    return jnp.where(active, values + orientation * 0.5 * (lower + upper), values)


def flat_sweep(values, layout, orientation):
    for stride, length in layout:
        for spacing in spacings(length, orientation):
            values = flat_level(values, stride, length, spacing, orientation)
    return values


def stencil_numbers(level_row, diffusion, courant):
    matches = (level_row[:, None] == (LOW + jnp.arange(4, dtype=jnp.int32))[None, :]).astype(
        jnp.float32
    )
    local_diff = jnp.sum(diffusion[2:, None] * matches, axis=0)
    local_cour = jnp.sum(courant[2:, None] * matches, axis=0)
    return (
        jnp.concatenate([diffusion[:2], local_diff]),
        jnp.concatenate([courant[:2], local_cour]),
    )


def subspace_map(level_row):
    side_len = 2**LOW
    entries = side_len**4
    flat_ids = jnp.arange(entries, dtype=jnp.int32)
    target = jnp.zeros((entries,), jnp.int32)
    for physical in range(4):
        digits = flat_ids // side_len ** (3 - physical) % side_len
        stored = level_row[physical] - LOW
        target = target + digits * jnp.power(side_len, 3 - stored).astype(jnp.int32)
    return (flat_ids[:, None] == target[None, :]).astype(jnp.float32)


def fine_layout(local_len):
    side_len = 2**LOW
    return [
        (local_len // side_len, side_len),
        (32 * side_len * side_len, 2 * side_len),
        (8 * side_len, 4 * side_len),
        (1, 8 * side_len),
    ]


def advance_rows(extended, diff_num, cour_num):
    center = extended[1:-1]
    forward_rows = extended[2:]
    backward_rows = extended[:-2]
    update = diff_num[0] * (forward_rows + backward_rows - 2.0 * center) - 0.5 * cour_num[0] * (
        forward_rows - backward_rows
    )
    forward = jnp.roll(center, -1, 1)
    backward = jnp.roll(center, 1, 1)
    update = (
        update
        + diff_num[1] * (forward + backward - 2.0 * center)
        - 0.5 * cour_num[1] * (forward - backward)
    )
    for offset, (stride, length) in enumerate(fine_layout(center.shape[-1])):
        forward = flat_forward(center, stride, length, 1)
        backward = flat_backward(center, stride, length, 1)
        update = (
            update
            + diff_num[2 + offset] * (forward + backward - 2.0 * center)
            - 0.5 * cour_num[2 + offset] * (forward - backward)
        )
    return center + update


def coarse_selector(fine_cols):
    side_len = 2**LOW
    coarse_ids = jnp.arange(side_len**3, dtype=jnp.int32)
    first = coarse_ids // (side_len * side_len)
    middle = coarse_ids // side_len % side_len
    last = coarse_ids % side_len
    target = 2 * first * 32 * side_len * side_len + 4 * middle * 8 * side_len + 8 * last
    fine_ids = jnp.arange(fine_cols, dtype=jnp.int32)
    return (fine_ids[:, None] == target[None, :]).astype(jnp.float32)


def linear_spread(ratio):
    side_len = 2**LOW
    fine_ids = jnp.arange(ratio * side_len, dtype=jnp.int32)
    coarse_ids = jnp.arange(side_len, dtype=jnp.int32)
    gap = (fine_ids[None, :] - ratio * coarse_ids[:, None]) % (ratio * side_len)
    reach = jnp.minimum(gap, ratio * side_len - gap).astype(jnp.float32)
    return jnp.maximum(1.0 - reach / float(ratio), 0.0)


def spread_table(fine_cols):
    table = jnp.einsum("ad,be,cf->abcdef", linear_spread(2), linear_spread(4), linear_spread(8))
    return table.reshape(-1, fine_cols)


def local(state_field, level_vectors, combine_weights, diffusion, courant):
    values = state_field[0]
    row_count = values.shape[0]
    second_len = values.shape[1]
    local_len = values.shape[2]
    side_len = 2**LOW
    fine_cols = local_len // side_len
    diff_num, cour_num = stencil_numbers(level_vectors[0], diffusion, courant)
    extended = with_halo(values, (("dom", 0),), 2)
    for repeat in range(2):
        extended = advance_rows(extended, diff_num, cour_num)
    values = extended
    coarse_layout = [
        (side_len**3, side_len),
        (side_len**2, side_len),
        (side_len, side_len),
        (1, side_len),
    ]
    selector = coarse_selector(fine_cols)
    coarse = jnp.dot(
        values.reshape(row_count * second_len * side_len, fine_cols),
        selector,
        precision=lax.Precision.HIGHEST,
    )
    coarse = coarse.reshape(row_count, second_len * side_len**4)
    coarse = flat_sweep(coarse, coarse_layout, -1.0)
    mapping = subspace_map(level_vectors[0])
    shared = coarse.reshape(row_count * second_len, side_len**4)
    weighted = combine_weights[0].astype(jnp.float32) * jnp.dot(
        shared, mapping, precision=lax.Precision.HIGHEST
    )
    combined = lax.psum(weighted, "grid")
    returned = jnp.dot(combined, mapping.T, precision=lax.Precision.HIGHEST)
    change = returned.reshape(row_count, -1) - coarse
    change = flat_sweep(change, coarse_layout, 1.0)
    spread = jnp.dot(
        change.reshape(row_count * second_len * side_len, side_len**3),
        spread_table(fine_cols),
        precision=lax.Precision.HIGHEST,
    )
    result = values + spread.reshape(row_count, second_len, local_len)
    return result.reshape(1, row_count, second_len, local_len)


def solution(mesh):
    placed = (P("grid", "dom", None, None), P("grid", None), P("grid"), P(), P())
    return jax.shard_map(
        local, mesh=mesh, in_specs=placed, out_specs=P("grid", "dom", None, None), check_vma=False
    )
```

profile of v0, /device:TPU:0, one launch (start us, length us, event | category | flops | bytes accessed | tf_op | source)
XLA Modules:
  0.0 142.0 jit_solution(15681989319254752497)
XLA Ops:
  0.5 4.0 %collective-permute-start.1 = (f32[2,8,16384]{2,1,0:T(8,128)}, f32[2,8,16384]{2,1,0:T(8,128)S(1)}, u32[]{:S(2)}, u32[]{:S(2)}) collective-permute-start(f32[2,8,16384]{2,1,0:T(8,128)} %bitcast.724), channel_id=1, source_target_pairs={{1,0},{2,1},{3,2},{4,3},{5,4},{6,5},{7,6},{0,7},{9,8},{10,9},{11,1... | collective-permute-start | bytes 3145736 | tf_op jit(solution)/shard_map/ppermute | solution.py:17
  5.2 1.4 fusion.349
  7.3 1.4 fusion.348
  12.3 1.5 %fusion.347 = (s32[1,1]{1,0:T(1,128)}, s32[1,1]{1,0:T(1,128)}, s32[1,1]{1,0:T(1,128)}, s32[1,1]{1,0:T(1,128)}) fusion(s32[1,4]{1,0:T(1,128)} %param.6), kind=kLoop, calls=%fused_computation.736 | loop fusion | bytes 32 | tf_op jit(solution)/shard_map/slice | solution.py:79
  30.8 0.7 fusion.236
  32.3 2.6 %multiply_bitcast_fusion = f32[4,4,4,8,16,32]{5,4,3,2,1,0:T(8,128)} fusion(f32[4,32]{1,0:T(4,128)S(1)} %fusion.252, f32[4,16,4,8]{1,3,0,2:T(8,128)S(1)} %broadcast_multiply_fusion), kind=kLoop, calls=%fused_computation | loop fusion | flops 262144 | bytes 1057280 | tf_op jit(solution)/shard_map/ad,be,cf->abcdef/transpose | solution.py:140
  40.5 4.4 %reshape.586 = f32[64,4096]{1,0:T(8,128)} reshape(f32[4,4,4,8,16,32]{5,4,3,2,1,0:T(8,128)} %multiply_bitcast_fusion) | data formatting | bytes 2097152 | tf_op jit(solution)/shard_map/reshape | solution.py:141
  47.1 0.8 copy-done.2
  49.2 2.1 %fusion.281 = (f32[4,8,16353]{2,1,0:T(8,128)S(1)}, f32[4,8,16353]{2,1,0:T(8,128)}) fusion(f32[6,8,16384]{2,1,0:T(8,128)S(1)} %pad_maximum_fusion), kind=kLoop, calls=%fused_computation.670 | loop fusion | bytes 8372736 | tf_op jit(solution)/shard_map/jit(_roll_static)/slice | solution.py:40
  51.2 2.6 %fusion.282 = (f32[4,8,16383]{2,1,0:T(8,128)}, f32[4,8,16383]{2,1,0:T(8,128)}) fusion(f32[6,8,16384]{2,1,0:T(8,128)S(1)} %pad_maximum_fusion), kind=kLoop, calls=%fused_computation.671 | loop fusion | bytes 8388096 | tf_op jit(solution)/shard_map/jit(_roll_static)/slice | solution.py:41
  53.9 2.6 %fusion.279 = (f32[4,8,15904]{2,1,0:T(8,128)}, f32[4,8,15904]{2,1,0:T(8,128)}) fusion(f32[6,8,16384]{2,1,0:T(8,128)S(1)} %pad_maximum_fusion), kind=kLoop, calls=%fused_computation.668 | loop fusion | bytes 8142848 | tf_op jit(solution)/shard_map/jit(_roll_static)/slice | solution.py:40
  56.5 2.2 %fusion.278 = (f32[4,8,15872]{2,1,0:T(8,128)}, f32[4,8,15872]{2,1,0:T(8,128)}) fusion(f32[6,8,16384]{2,1,0:T(8,128)S(1)} %pad_maximum_fusion), kind=kLoop, calls=%fused_computation.667 | loop fusion | bytes 8126464 | tf_op jit(solution)/shard_map/jit(_roll_static)/slice | solution.py:41
  58.6 1.9 %fusion.276 = (f32[4,8,12800]{2,1,0:T(8,128)}, f32[4,8,12800]{2,1,0:T(8,128)}) fusion(f32[6,8,16384]{2,1,0:T(8,128)S(1)} %pad_maximum_fusion), kind=kLoop, calls=%fused_computation.665 | loop fusion | bytes 6553600 | tf_op jit(solution)/shard_map/jit(_roll_static)/slice | solution.py:40
  60.6 1.9 %fusion.274 = (f32[4,8,12288]{2,1,0:T(8,128)}, f32[4,8,12288]{2,1,0:T(8,128)}) fusion(f32[6,8,16384]{2,1,0:T(8,128)S(1)} %pad_maximum_fusion), kind=kLoop, calls=%fused_computation.663 | loop fusion | bytes 6291456 | tf_op jit(solution)/shard_map/jit(_roll_static)/slice | solution.py:33
  62.5 1.1 fusion.275
  63.6 1.0 fusion.277
  64.6 1.0 fusion.273
  65.6 19.7 %subtract_add_fusion = f32[4,8,16384]{2,1,0:T(8,128)S(1)} fusion(f32[2,8,16384]{2,1,0:T(8,128)} %copy-done.3, f32[2,8,16384]{2,1,0:T(8,128)} %bitcast.725, f32[2,8,16384]{2,1,0:T(8,128)} %copy-done.2, f32[4,8,16383]{2,1,0:T(8,128)} %get-tuple-element.78, f32[4,8,16353]{2,1,0:T(8,128)} %get-tuple-element.76, f32[4,8,16383]{2,1,0:T(8,128)} %get-tuple-element.77, ...), kind=kLoop, calls=%fused_computation.45 | loop fusion | flops 45613056 | bytes 40722480 | tf_op jit(solution)/shard_map/add | solution.py:116
  87.8 10.0 %subtract_add_fusion.1 = f32[2,8,16384]{2,1,0:T(8,128)S(1)} fusion(f32[2,8,16383]{2,1,0:T(8,128)S(1)} %get-tuple-element.108, f32[2,8,1]{2,1,0:T(8,128)S(1)} %get-tuple-element.110, f32[2,8,31]{2,1,0:T(8,128)S(1)} %get-tuple-element.104, f32[2,8,16353]{2,1,0:T(8,128)S(1)} %get-tuple-element.106, f32[2,8,1]{2,1,0:T(8,128)S(1)} %get-tuple-element.109, ...), kind=kLoop, calls=%fused_computation.75 | loop fusion | flops 17039360 | bytes 21069872 | tf_op jit(solution)/shard_map/add | solution.py:116
  98.7 1.0 fusion.27
  103.6 16.6 %psum.7 = f32[16,256]{1,0:T(8,128)S(1)} all-reduce(f32[16,256]{1,0:T(8,128)S(1)} %convolution_multiply_fusion), channel_id=1, replica_groups=mesh['grid'=4,'dom'=8] {'grid'}, use_global_device_ids=true, to_apply=%region_2.3 | all-reduce | flops 4096 | bytes 32768 | tf_op jit(solution)/shard_map/psum | solution.py:175
  121.5 0.7 add_select_fusion.26
  128.9 0.8 concatenate.595
  129.7 1.4 concatenate.585
  131.1 1.4 concatenate.587
  132.6 1.4 concatenate.589
  134.0 1.4 %concatenate.591 = f32[64,64]{1,0:T(8,128)} reshape(f32[2,2048]{1,0:T(2,128)} %get-tuple-element.29) | data formatting | bytes 32768 | tf_op jit(solution)/shard_map/jit(_roll_static)/concatenate | solution.py:34
  135.4 1.4 concatenate.581
  136.8 1.4 concatenate.583
  138.2 1.1 add_select_fusion.5
  139.4 1.0 fusion.352
  140.9 1.1 add_bitcast_fusion
  (310 shorter events, 39.8 us)
Async XLA Ops:
  0.0 46.9 %collective-permute-start = (f32[2,8,16384]{2,1,0:T(8,128)}, f32[2,8,16384]{2,1,0:T(8,128)S(1)}, u32[]{:S(2)}, u32[]{:S(2)}) collective-permute-start(f32[2,8,16384]{2,1,0:T(8,128)} %bitcast.723), channel_id=1, source_target_pairs={{0,1},{1,2},{2,3},{3,4},{4,5},{5,6},{6,7},{7,0},{8,9},{9,10},{10,1... | collective-permute-start | bytes 3145736 | tf_op jit(solution)/shard_map/ppermute | solution.py:16
  0.5 46.5 %collective-permute-start.1 = (f32[2,8,16384]{2,1,0:T(8,128)}, f32[2,8,16384]{2,1,0:T(8,128)S(1)}, u32[]{:S(2)}, u32[]{:S(2)}) collective-permute-start(f32[2,8,16384]{2,1,0:T(8,128)} %bitcast.724), channel_id=1, source_target_pairs={{1,0},{2,1},{3,2},{4,3},{5,4},{6,5},{7,6},{0,7},{9,8},{10,9},{11,1... | collective-permute-start | bytes 3145736 | tf_op jit(solution)/shard_map/ppermute | solution.py:17
  8.8 91.8 %copy-start.4 = (pred[2048]{0:T(1024)(128)(4,1)}, pred[2048]{0:T(1024)(128)(4,1)S(1)}, u32[]{:S(2)}) copy-start(pred[2048]{0:T(1024)(128)(4,1)S(1)} %get-tuple-element.244) | copy-start | bytes 6148
  8.8 91.8 %copy-start.6 = (pred[2048]{0:T(1024)(128)(4,1)}, pred[2048]{0:T(1024)(128)(4,1)S(1)}, u32[]{:S(2)}) copy-start(pred[2048]{0:T(1024)(128)(4,1)S(1)} %broadcast_compare_fusion.26) | copy-start | bytes 6148
  40.5 6.4 %copy-start.1 = (f32[1,2,8,16384]{3,2,1,0:T(8,128)S(1)}, f32[1,2,8,16384]{3,2,1,0:T(8,128)}, u32[]{:S(2)}) copy-start(f32[1,2,8,16384]{3,2,1,0:T(8,128)} %param.5) | copy-start | bytes 3145732
  98.5 4.6 %copy-start.24 = (pred[8,256]{1,0:T(8,128)(4,1)S(1)}, pred[8,256]{1,0:T(8,128)(4,1)}, u32[]{:S(2)}) copy-start(pred[8,256]{1,0:T(8,128)(4,1)} %get-tuple-element.257) | copy-start | bytes 6148
  98.5 4.6 %copy-start.25 = (pred[8,256]{1,0:T(8,128)(4,1)S(1)}, pred[8,256]{1,0:T(8,128)(4,1)}, u32[]{:S(2)}) copy-start(pred[8,256]{1,0:T(8,128)(4,1)} %get-tuple-element.258) | copy-start | bytes 6148
  98.5 4.6 %copy-start.26 = (pred[8,256]{1,0:T(8,128)(4,1)S(1)}, pred[8,256]{1,0:T(8,128)(4,1)}, u32[]{:S(2)}) copy-start(pred[8,256]{1,0:T(8,128)(4,1)} %get-tuple-element.259) | copy-start | bytes 6148
  98.5 4.6 %copy-start.27 = (pred[8,256]{1,0:T(8,128)(4,1)S(1)}, pred[8,256]{1,0:T(8,128)(4,1)}, u32[]{:S(2)}) copy-start(pred[8,256]{1,0:T(8,128)(4,1)} %get-tuple-element.260) | copy-start | bytes 6148
  98.5 4.6 %copy-start.28 = (pred[8,256]{1,0:T(8,128)(4,1)S(1)}, pred[8,256]{1,0:T(8,128)(4,1)}, u32[]{:S(2)}) copy-start(pred[8,256]{1,0:T(8,128)(4,1)} %get-tuple-element.261) | copy-start | bytes 6148
  98.5 4.6 %copy-start.29 = (pred[8,256]{1,0:T(8,128)(4,1)S(1)}, pred[8,256]{1,0:T(8,128)(4,1)}, u32[]{:S(2)}) copy-start(pred[8,256]{1,0:T(8,128)(4,1)} %get-tuple-element.262) | copy-start | bytes 6148
  98.5 4.6 %copy-start.30 = (pred[8,256]{1,0:T(8,128)(4,1)S(1)}, pred[8,256]{1,0:T(8,128)(4,1)}, u32[]{:S(2)}) copy-start(pred[8,256]{1,0:T(8,128)(4,1)} %get-tuple-element.263) | copy-start | bytes 6148
  98.6 4.6 %copy-start.31 = (pred[8,256]{1,0:T(8,128)(4,1)S(1)}, pred[8,256]{1,0:T(8,128)(4,1)}, u32[]{:S(2)}) copy-start(pred[8,256]{1,0:T(8,128)(4,1)} %get-tuple-element.264) | copy-start | bytes 6148
  98.6 4.6 %copy-start.32 = (pred[8,256]{1,0:T(8,128)(4,1)S(1)}, pred[8,256]{1,0:T(8,128)(4,1)}, u32[]{:S(2)}) copy-start(pred[8,256]{1,0:T(8,128)(4,1)} %get-tuple-element.265) | copy-start | bytes 6148
  98.6 4.6 %copy-start.33 = (pred[8,256]{1,0:T(8,128)(4,1)S(1)}, pred[8,256]{1,0:T(8,128)(4,1)}, u32[]{:S(2)}) copy-start(pred[8,256]{1,0:T(8,128)(4,1)} %get-tuple-element.266) | copy-start | bytes 6148
  98.6 4.6 %copy-start.34 = (pred[8,256]{1,0:T(8,128)(4,1)S(1)}, pred[8,256]{1,0:T(8,128)(4,1)}, u32[]{:S(2)}) copy-start(pred[8,256]{1,0:T(8,128)(4,1)} %get-tuple-element.267) | copy-start | bytes 6148
  98.6 4.6 %copy-start.35 = (pred[8,256]{1,0:T(8,128)(4,1)S(1)}, pred[8,256]{1,0:T(8,128)(4,1)}, u32[]{:S(2)}) copy-start(pred[8,256]{1,0:T(8,128)(4,1)} %get-tuple-element.268) | copy-start | bytes 6148
  98.6 4.6 %copy-start.36 = (pred[8,256]{1,0:T(8,128)(4,1)S(1)}, pred[8,256]{1,0:T(8,128)(4,1)}, u32[]{:S(2)}) copy-start(pred[8,256]{1,0:T(8,128)(4,1)} %get-tuple-element.269) | copy-start | bytes 6148
  98.6 4.6 %copy-start.37 = (pred[8,256]{1,0:T(8,128)(4,1)S(1)}, pred[8,256]{1,0:T(8,128)(4,1)}, u32[]{:S(2)}) copy-start(pred[8,256]{1,0:T(8,128)(4,1)} %get-tuple-element.270) | copy-start | bytes 6148
  98.6 4.6 %copy-start.38 = (pred[8,256]{1,0:T(8,128)(4,1)S(1)}, pred[8,256]{1,0:T(8,128)(4,1)}, u32[]{:S(2)}) copy-start(pred[8,256]{1,0:T(8,128)(4,1)} %get-tuple-element.271) | copy-start | bytes 6148
  98.6 4.6 %copy-start.39 = (pred[8,256]{1,0:T(8,128)(4,1)S(1)}, pred[8,256]{1,0:T(8,128)(4,1)}, u32[]{:S(2)}) copy-start(pred[8,256]{1,0:T(8,128)(4,1)} %get-tuple-element.272) | copy-start | bytes 6148
  98.7 4.6 %copy-start.40 = (pred[8,256]{1,0:T(8,128)(4,1)S(1)}, pred[8,256]{1,0:T(8,128)(4,1)}, u32[]{:S(2)}) copy-start(pred[8,256]{1,0:T(8,128)(4,1)} %get-tuple-element.273) | copy-start | bytes 6148
  98.7 4.6 %copy-start.41 = (pred[8,256]{1,0:T(8,128)(4,1)S(1)}, pred[8,256]{1,0:T(8,128)(4,1)}, u32[]{:S(2)}) copy-start(pred[8,256]{1,0:T(8,128)(4,1)} %get-tuple-element.274) | copy-start | bytes 6148
  98.7 4.6 %copy-start.42 = (pred[8,256]{1,0:T(8,128)(4,1)S(1)}, pred[8,256]{1,0:T(8,128)(4,1)}, u32[]{:S(2)}) copy-start(pred[8,256]{1,0:T(8,128)(4,1)} %get-tuple-element.275) | copy-start | bytes 6148
  98.7 4.6 %copy-start.43 = (pred[8,256]{1,0:T(8,128)(4,1)S(1)}, pred[8,256]{1,0:T(8,128)(4,1)}, u32[]{:S(2)}) copy-start(pred[8,256]{1,0:T(8,128)(4,1)} %get-tuple-element.276) | copy-start | bytes 6148
  98.7 4.6 %copy-start.44 = (s32[256]{0:T(256)S(1)}, s32[256]{0:T(256)}, u32[]{:S(2)}) copy-start(s32[256]{0:T(256)} %fusion.255) | copy-start | bytes 3076
  98.7 21.7 %copy-start.8 = (pred[2048]{0:T(1024)(128)(4,1)S(1)}, pred[2048]{0:T(1024)(128)(4,1)}, u32[]{:S(2)}) copy-start(pred[2048]{0:T(1024)(128)(4,1)} %get-tuple-element.277) | copy-start | bytes 6148
  98.7 21.7 %copy-start.9 = (pred[2048]{0:T(1024)(128)(4,1)S(1)}, pred[2048]{0:T(1024)(128)(4,1)}, u32[]{:S(2)}) copy-start(pred[2048]{0:T(1024)(128)(4,1)} %get-tuple-element.278) | copy-start | bytes 6148
  98.7 21.7 %copy-start.10 = (pred[2048]{0:T(1024)(128)(4,1)S(1)}, pred[2048]{0:T(1024)(128)(4,1)}, u32[]{:S(2)}) copy-start(pred[2048]{0:T(1024)(128)(4,1)} %fusion.197) | copy-start | bytes 6148
  100.7 22.7 %copy-start.5 = (pred[2048]{0:T(1024)(128)(4,1)S(1)}, pred[2048]{0:T(1024)(128)(4,1)}, u32[]{:S(2)}) copy-start(pred[2048]{0:T(1024)(128)(4,1)} %copy-done.4) | copy-start | bytes 6148
  100.7 22.7 %copy-start.7 = (pred[2048]{0:T(1024)(128)(4,1)S(1)}, pred[2048]{0:T(1024)(128)(4,1)}, u32[]{:S(2)}) copy-start(pred[2048]{0:T(1024)(128)(4,1)} %copy-done.6) | copy-start | bytes 6148
  125.2 14.2 %copy-start = (f32[64,4096]{1,0:T(8,128)S(1)}, f32[64,4096]{1,0:T(8,128)}, u32[]{:S(2)}) copy-start(f32[64,4096]{1,0:T(8,128)} %reshape.586) | copy-start | bytes 3145732
  (16 other events, 54.4 us)
where the time goes:
time: 143 us; the launch traced here: 142 us
  other arithmetic  60.3 us (42%)
  local copies, waits for them, and re-layouts  49.9 us (35%)
  blocking collectives  16.6 us (12%)
  between operations  8.29 us (6%)
  starting transfers between devices  4.49 us (3%)
  matrix products  2.39 us (2%)
    add x2, other arithmetic, advance_rows(): return center + update  29.8 us
    psum x1, blocking collectives, local(): combined = lax.psum(weighted, 'grid')  16.6 us
    lt x20, other arithmetic, flat_backward(): return jnp.where(digit < distance, wrapped, plain)  8.47 us
    slice x10, local copies, waits for them, and re-layouts, flat_backward(): wrapped = jnp.roll(values, -(length - distance) * stride, -1)  7.8 us
    eq x16, other arithmetic, flat_level(): active = digit % (2 * spacing) == spacing  7.38 us
    slice x13, local copies, waits for them, and re-layouts, flat_backward(): plain = jnp.roll(values, distance * stride, -1)  6.21 us
    slice x26, local copies, waits for them, and re-layouts, flat_forward(): wrapped = jnp.roll(values, (length - distance) * stride, -1)  5.36 us
    concatenate x24, local copies, waits for them, and re-layouts, flat_backward(): plain = jnp.roll(values, distance * stride, -1)  4.95 us
  transfers between devices with their start and end apart: 2, of which 0 were waited for; matrix products, arithmetic and copies ran while one was open for 25% of the time, Pallas kernels for 0%

commit v1 on v0

v1 whole, which is shorter than its diff:
```python
import functools

import jax
import jax.numpy as jnp
import numpy as np
from jax import lax
from jax.experimental import pallas as pl
from jax.experimental.pallas import tpu as pltpu
from jax.sharding import PartitionSpec as P

LOW = 2
SIDE = 2**LOW
COARSE = SIDE**4
LANES = 128
GROUP = 16 * SIDE * SIDE * 2
MESH = pl.DeviceIdType.MESH


def level_matrix(length, orientation):
    ladder = [2**e for e in range(length.bit_length() - 1)]
    total = np.eye(length)
    for h in ladder if orientation < 0 else ladder[::-1]:
        step = np.eye(length)
        for i in range(h, length, 2 * h):
            step[i, (i - h) % length] += 0.5 * orientation
            step[i, (i + h) % length] += 0.5 * orientation
        total = step @ total
    return total


def kron4(m):
    return np.kron(np.kron(np.kron(m, m), m), m)


def packed_order():
    p = np.arange(COARSE)
    tile = p // LANES * 32 + p % LANES // 32 * 8 + p % 8
    return tile * 4 + p % 32 // 8


def interpolation(ratio):
    fine = np.arange(ratio * SIDE)
    gap = (fine[None, :] - ratio * np.arange(SIDE)[:, None]) % (ratio * SIDE)
    reach = np.minimum(gap, ratio * SIDE - gap)
    return np.maximum(1.0 - reach / ratio, 0.0)


def constant_table():
    down = kron4(level_matrix(SIDE, -1.0)).T[packed_order()]
    up = kron4(level_matrix(SIDE, 1.0)).T
    spread = np.kron(interpolation(4), interpolation(8))
    spread = np.tile(spread, (COARSE // spread.shape[0], 1))
    return np.concatenate([down, up, spread], axis=1).astype(jnp.bfloat16)


def parts_of(x):
    high = x.astype(jnp.bfloat16)
    rest = x - high.astype(jnp.float32)
    mid = rest.astype(jnp.bfloat16)
    low = (rest - mid.astype(jnp.float32)).astype(jnp.bfloat16)
    return high, mid, low


def exact_dot(x, table):
    high, mid, low = parts_of(x)
    dot = functools.partial(jnp.dot, preferred_element_type=jnp.float32)
    return dot(high, table) + (dot(mid, table) + dot(low, table))


def kernel(
    grids, doms, chunks,
    level_ref, weight_ref, diff_ref, cour_ref, state_ref, table_hbm,
    out_ref,
    u, w, acc, near, far, mine, table, c_out, c_in, g_out, g_in, z,
    in_sem, raw_s, raw_r, far_s, far_r, cs, cr, gs, gr, out_sem,
):
    rows, second, cells = u.shape
    gi, di = lax.axis_index("grid"), lax.axis_index("dom")
    above, below = lax.rem(di + 1, doms), lax.rem(di + doms - 1, doms)
    peers = [lax.rem(gi + k, grids) for k in range(1, grids)]

    barrier = pltpu.get_barrier_semaphore()
    for side in (above, below):
        pl.semaphore_signal(barrier, inc=1, device_id=(gi, side), device_id_type=MESH)
    for peer in peers:
        pl.semaphore_signal(barrier, inc=1, device_id=(peer, di), device_id_type=MESH)
    load = pltpu.make_async_copy(state_ref.at[0], u, in_sem.at[0])
    load.start()
    load_table = pltpu.make_async_copy(table_hbm, table, in_sem.at[1])
    load_table.start()
    pl.semaphore_wait(barrier, 2 + len(peers))

    targets = ((gi, above), (gi, below))
    raw = []
    for s, row in ((0, rows - 1), (1, 0)):
        raw.append(
            pltpu.make_async_remote_copy(
                src_ref=state_ref.at[0, row], dst_ref=near.at[s],
                send_sem=raw_s.at[s], recv_sem=raw_r.at[s],
                device_id=targets[s], device_id_type=MESH,
            )
        )
        raw[-1].start()

    kappa, sigma = [diff_ref[0], diff_ref[1]], [cour_ref[0], cour_ref[1]]
    for j in range(4):
        k_sum, s_sum = jnp.float32(0.0), jnp.float32(0.0)
        for p in range(4):
            here = level_ref[0, p] == LOW + j
            k_sum = k_sum + jnp.where(here, diff_ref[2 + p], 0.0)
            s_sum = s_sum + jnp.where(here, cour_ref[2 + p], 0.0)
        kappa.append(k_sum)
        sigma.append(s_sum)
    a = [k - 0.5 * s for k, s in zip(kappa, sigma)]
    b = [k + 0.5 * s for k, s in zip(kappa, sigma)]
    centre = 1.0 - 2.0 * (kappa[0] + kappa[1] + kappa[2] + kappa[3] + kappa[4] + kappa[5])

    lane = lax.broadcasted_iota(jnp.int32, (second, LANES), 1)
    digit = lane % 32
    first_digit, last_digit = digit == 0, digit == 31
    in_low, in_high = lane < LANES - 32, lane >= 32
    tiles = GROUP // LANES
    outer = cells // GROUP
    n3 = 2 * SIDE
    n2 = outer // n3

    def neighbours(g):
        d2, d3 = g // n3, g % n3
        starts = []
        for e2, e3 in ((1, 0), (n2 - 1, 0), (0, 1), (0, n3 - 1)):
            starts.append(((d2 + e2) % n2 * n3 + (d3 + e3) % n3) * GROUP)
        return starts

    def apply_d(ref, r, g):
        here = g * GROUP
        n = neighbours(g)
        at = lambda start, t: ref[r, :, pl.ds(pl.multiple_of(start + t * LANES, LANES), LANES)]
        v = [at(here, t) for t in range(tiles)]
        ahead = [pltpu.roll(x, LANES - 32, 1) for x in v]
        behind = [pltpu.roll(x, 32, 1) for x in v]
        out = []
        for t, x in enumerate(v):
            y = centre * x
            y += a[1] * pltpu.roll(x, second - 1, 0) + b[1] * pltpu.roll(x, 1, 0)
            y += a[2] * at(n[0], t) + b[2] * at(n[1], t)
            y += a[3] * at(n[2], t) + b[3] * at(n[3], t)
            y += a[4] * jnp.where(in_low, ahead[t], ahead[(t + 1) % tiles])
            y += b[4] * jnp.where(in_high, behind[t], behind[(t - 1) % tiles])
            y += a[5] * jnp.where(last_digit, pltpu.roll(x, 31, 1), pltpu.roll(x, LANES - 1, 1))
            y += b[5] * jnp.where(first_digit, pltpu.roll(x, LANES - 31, 1), pltpu.roll(x, 1, 1))
            out.append(y)
        return v, out

    def spot(g, t):
        return pl.ds(pl.multiple_of(g * GROUP + t * LANES, LANES), LANES)

    load.wait()

    @pl.loop(0, outer)
    def _(g):
        us, ws = [], []
        for r in range(rows):
            v, y = apply_d(u, r, g)
            us.append(v)
            ws.append(y)
            for t in range(tiles):
                w[r, :, spot(g, t)] = y[t]
        for t in range(tiles):
            mine[0, :, spot(g, t)] = 2.0 * b[0] * ws[rows - 1][t] + b[0] * b[0] * us[rows - 2][t]
            mine[1, :, spot(g, t)] = 2.0 * a[0] * ws[0][t] + a[0] * a[0] * us[1][t]

    coarse_lane = (lane < 32) & (lane % 8 == 0)

    def pack(ref, r):
        halves = []
        for half in range(2):
            total = None
            for block in range(4):
                part = None
                for k in range(8):
                    i = half * 32 + block * 8 + k
                    start = (i // 16 * n3 + i // 4 % 4 * 2) * GROUP + i % 4 * LANES
                    x = jnp.where(coarse_lane, ref[r, :, start : start + LANES], 0.0)
                    x = x if k == 0 else pltpu.roll(x, k, 1)
                    part = x if part is None else part + x
                part = part if block == 0 else pltpu.roll(part, 32 * block, 1)
                total = part if total is None else total + part
            halves.append(total)
        return halves

    def store_pack(dst, slot, place, ref, r):
        low, high = pack(ref, r)
        dst[slot, place, :, 0:LANES] = low
        dst[slot, place, :, LANES : 2 * LANES] = high

    store_pack(c_out, 0, 0, u, rows - 1)
    store_pack(c_out, 0, 1, mine, 0)
    store_pack(c_out, 1, 0, u, 0)
    store_pack(c_out, 1, 1, mine, 1)

    coarse, bulk = [], []
    for s in range(2):
        coarse.append(
            pltpu.make_async_remote_copy(
                src_ref=c_out.at[s], dst_ref=c_in.at[s],
                send_sem=cs.at[s], recv_sem=cr.at[s],
                device_id=targets[s], device_id_type=MESH,
            )
        )
        coarse[-1].start()
    width = cells // chunks
    for c in range(chunks):
        for s in range(2):
            cut = (s, slice(None), pl.ds(c * width, width))
            bulk.append(
                pltpu.make_async_remote_copy(
                    src_ref=mine.at[cut], dst_ref=far.at[cut],
                    send_sem=far_s.at[s, c], recv_sem=far_r.at[s, c],
                    device_id=targets[s], device_id_type=MESH,
                )
            )
            bulk[-1].start()

    @pl.loop(0, outer)
    def _(g):
        for r in range(rows):
            _, y = apply_d(w, r, g)
            for t in range(tiles):
                x = y[t] + 2.0 * a[0] * b[0] * u[r, :, spot(g, t)]
                if r + 1 < rows:
                    x += 2.0 * a[0] * w[r + 1, :, spot(g, t)]
                if r >= 1:
                    x += 2.0 * b[0] * w[r - 1, :, spot(g, t)]
                if r + 2 < rows:
                    x += a[0] * a[0] * u[r + 2, :, spot(g, t)]
                if r >= 2:
                    x += b[0] * b[0] * u[r - 2, :, spot(g, t)]
                acc[r, :, spot(g, t)] = x

    scale = []
    for p in range(4):
        value = jnp.int32(0)
        for j in range(4):
            value = value + jnp.where(level_ref[0, p] == LOW + j, SIDE ** (3 - j), 0)
        scale.append(value)

    def placement(flat):
        target = jnp.zeros_like(flat)
        for p in range(4):
            target = target + flat // SIDE ** (3 - p) % SIDE * scale[p]
        return target

    row_id = lax.broadcasted_iota(jnp.int32, (COARSE, COARSE), 0)
    col_id = lax.broadcasted_iota(jnp.int32, (COARSE, COARSE), 1)
    one = lambda hit: jnp.where(hit, 1.0, 0.0).astype(jnp.bfloat16)
    forward = one(row_id == placement(col_id))
    backward = one(col_id == placement(row_id))

    pieces = [jnp.concatenate(pack(acc, r), axis=1) for r in range(rows)]
    for s in range(2):
        coarse[s].wait_recv()
    pieces[0] += c_in[0, 1]
    pieces[1] += b[0] * b[0] * c_in[0, 0]
    pieces[rows - 1] += c_in[1, 1]
    pieces[rows - 2] += a[0] * a[0] * c_in[1, 0]
    points = jnp.concatenate(pieces, axis=0)
    load_table.wait()
    surplus = exact_dot(points, table[:, 0:COARSE])
    weighted = weight_ref[0].astype(jnp.float32) * exact_dot(surplus, forward)
    g_out[...] = weighted
    shares = []
    for k, peer in enumerate(peers):
        shares.append(
            pltpu.make_async_remote_copy(
                src_ref=g_out, dst_ref=g_in.at[k],
                send_sem=gs.at[k], recv_sem=gr.at[k],
                device_id=(peer, di), device_id_type=MESH,
            )
        )
        shares[-1].start()
    combined = weighted
    for k in range(len(peers)):
        shares[k].wait_recv()
        combined = combined + g_in[k]
    change = exact_dot(combined, backward) - surplus
    change = exact_dot(change, table[:, COARSE : 2 * COARSE])

    per_group = 16
    for g in range(COARSE // per_group):
        half, place = g * per_group // LANES, g % (LANES // per_group)
        x = change[:, half * LANES : (half + 1) * LANES]
        block = lax.broadcasted_iota(jnp.int32, x.shape, 1) // per_group
        x = jnp.where(block == place, x, 0.0)
        z[g] = exact_dot(x, table[0:LANES, 2 * COARSE :])

    for s in range(2):
        raw[s].wait_recv()

    @pl.loop(0, outer // 2)
    def _(i):
        d2, c3 = i // SIDE, i % SIDE
        after = d2 * SIDE + (c3 + 1) % SIDE
        for r in range(rows):
            for t in range(tiles):
                cut = (pl.ds(r * second, second), slice(t * LANES, (t + 1) * LANES))
                even = z[(i,) + cut]
                odd = 0.5 * (even + z[(after,) + cut])
                for h, x in ((0, even), (1, odd)):
                    if r == 1:
                        x += b[0] * b[0] * near[0, :, spot(2 * i + h, t)]
                    if r == rows - 2:
                        x += a[0] * a[0] * near[1, :, spot(2 * i + h, t)]
                    acc[r, :, spot(2 * i + h, t)] += x

    saves = []
    for c in range(chunks):
        for s in range(2):
            bulk[2 * c + s].wait_recv()

        @pl.loop(0, width // GROUP)
        def _(i):
            for t in range(tiles):
                here = spot(c * (width // GROUP) + i, t)
                acc[0, :, here] += far[0, :, here]
                acc[rows - 1, :, here] += far[1, :, here]

        cut = (slice(None), slice(None), pl.ds(c * width, width))
        saves.append(pltpu.make_async_copy(acc.at[cut], out_ref.at[(0,) + cut], out_sem.at[c]))
        saves[-1].start()
    for copy in raw + coarse + bulk + shares:
        copy.wait_send()
    for copy in saves:
        copy.wait()


def local(grids, doms, state_field, level_vectors, combine_weights, diffusion, courant):
    _, rows, second, cells = state_field.shape
    chunks = 4
    table = jnp.asarray(constant_table())
    f32 = jnp.float32
    dma = pltpu.SemaphoreType.DMA
    smem = pl.BlockSpec(memory_space=pltpu.SMEM)
    anywhere = pl.BlockSpec(memory_space=pl.ANY)
    others = max(grids - 1, 1)
    return pl.pallas_call(
        functools.partial(kernel, grids, doms, chunks),
        out_shape=jax.ShapeDtypeStruct(state_field.shape, f32),
        in_specs=[smem] * 4 + [anywhere] * 2,
        out_specs=anywhere,
        scratch_shapes=[
            pltpu.VMEM((rows, second, cells), f32),
            pltpu.VMEM((rows, second, cells), f32),
            pltpu.VMEM((rows, second, cells), f32),
            pltpu.VMEM((2, second, cells), f32),
            pltpu.VMEM((2, second, cells), f32),
            pltpu.VMEM((2, second, cells), f32),
            pltpu.VMEM(table.shape, jnp.bfloat16),
            pltpu.VMEM((2, 2, second, COARSE), f32),
            pltpu.VMEM((2, 2, second, COARSE), f32),
            pltpu.VMEM((rows * second, COARSE), f32),
            pltpu.VMEM((others, rows * second, COARSE), f32),
            pltpu.VMEM((SIDE * SIDE, rows * second, GROUP), f32),
            dma((2,)),
            dma((2,)),
            dma((2,)),
            dma((2, chunks)),
            dma((2, chunks)),
            dma((2,)),
            dma((2,)),
            dma((others,)),
            dma((others,)),
            dma((chunks,)),
        ],
        compiler_params=pltpu.CompilerParams(
            collective_id=0, has_side_effects=True, vmem_limit_bytes=40 * 2**20
        ),
    )(level_vectors, combine_weights, diffusion, courant, state_field, table)


def solution(mesh):
    placed = (P("grid", "dom", None, None), P("grid", None), P("grid"), P(), P())
    return jax.shard_map(
        functools.partial(local, mesh.shape["grid"], mesh.shape["dom"]),
        mesh=mesh,
        in_specs=placed,
        out_specs=P("grid", "dom", None, None),
        check_vma=False,
    )
```

time: 143 us -> 34.8 us (0.24)
  other arithmetic: 60.3 us -> 0 us
  local copies, waits for them, and re-layouts: 49.9 us -> 3.24 us
  Pallas kernels: 0 us -> 30.7 us
  blocking collectives: 16.6 us -> 0 us
  between operations: 8.29 us -> 0.74 us
  starting transfers between devices: 4.49 us -> 0 us
  matrix products: 2.39 us -> 0 us
    add x5 -> x0, other arithmetic: 30.9 us -> none  [the longest x2 29.8 us: advance_rows(): return center + update]
    pallas_call x0 -> x1, Pallas kernels: none -> 30.7 us  [local(): pl.pallas_call(functools.partial(kernel, grids, doms, chunks), out_shape=...]
    slice x81 -> x0, local copies, waits for them, and re-layouts: 29.5 us -> none  [the longest x10 7.8 us: flat_backward(): wrapped = jnp.roll(values, -(length - distance) * stride, -1)]
    psum x1 -> x0, blocking collectives: 16.6 us -> none  [local(): combined = lax.psum(weighted, 'grid')]
    concatenate x72 -> x0, local copies, waits for them, and re-layouts: 13.4 us -> none  [the longest x24 4.95 us: flat_backward(): plain = jnp.roll(values, distance * stride, -1)]
    lt x20 -> x0, other arithmetic: 8.47 us -> none  [flat_backward(): return jnp.where(digit < distance, wrapped, plain)]
    eq x16 -> x0, other arithmetic: 7.38 us -> none  [flat_level(): active = digit % (2 * spacing) == spacing]
    reshape x7 -> x0, local copies, waits for them, and re-layouts: 5.48 us -> none  [the longest x1 4.4 us: spread_table(): return table.reshape(-1, fine_cols)]
  transfers between devices with their start and end apart: 2 -> 0, of which waited for: 0 -> 0; matrix products, arithmetic and copies ran while one was open for 25% -> 0% of each run, Pallas kernels for 0% -> 0%
where the time goes in v1:
time: 34.8 us; the launch traced here: 34.6 us
  Pallas kernels  30.7 us (88%)
  local copies, waits for them, and re-layouts  3.24 us (9%)
  between operations  0.74 us (2%)
    pallas_call x1, Pallas kernels, local(): pl.pallas_call(functools.partial(kernel, grids, doms, chunks), out_shape=...  30.7 us
    unnamed x11, local copies, waits for them, and re-layouts  3.24 us

profile of v1, /device:TPU:0, one launch (start us, length us, event | category | flops | bytes accessed | tf_op | source)
XLA Modules:
  0.0 34.6 jit_solution(5499626914002907630)
XLA Ops:
  0.0 0.0 copy-start.4
  0.0 0.0 copy-start.3
  0.0 0.0 copy-start.2
  0.7 0.0 copy-done.4
  0.7 0.0 copy-done.3
  0.7 0.0 copy-done.2
  0.7 0.0 copy-start
  0.7 1.2 %copy-done = f32[1,2,8,16384]{3,2,1,0:T(8,128)S(1)} copy-done((f32[1,2,8,16384]{3,2,1,0:T(8,128)S(1)}, f32[1,2,8,16384]{3,2,1,0:T(8,128)}, u32[]{:S(2)}) %copy-start) | copy-done | bytes 1048600
  2.0 0.0 copy-start.1
  2.0 1.0 %copy-done.1 = bf16[256,1024]{1,0:T(8,128)(2,1)S(1)} copy-done((bf16[256,1024]{1,0:T(8,128)(2,1)S(1)}, bf16[256,1024]{1,0:T(8,128)(2,1)}, u32[]{:S(2)}) %copy-start.1) | copy-done | bytes 524312
  3.0 30.7 %shard_map.64 = f32[1,2,8,16384]{3,2,1,0:T(8,128)S(1)} custom-call(s32[1,4]{1,0:T(1,128)S(1)} %copy-done.2, s32[1]{0:T(128)S(6)} %copy.8.weight_ref, f32[6]{0:T(128)S(1)} %copy-done.3, f32[6]{0:T(128)S(1)} %copy-done.4, f32[1,2,8,16384]{3,2,1,0:T(8,128)S(1)} %copy-done, bf16[256,1024]{1,0:T(8,128)(2,1)S(1)} %copy-done.1), custom_call_target="tpu_custom_call" | custom-call | tf_op jit(solution)/shard_map/pallas_call | solution.py:345
  33.7 1.0 %copy.9 = f32[1,2,8,16384]{3,2,1,0:T(8,128)} copy(f32[1,2,8,16384]{3,2,1,0:T(8,128)S(1)} %shard_map.64) | data formatting | bytes 2097152
Async XLA Ops:
  0.0 0.7 %copy-start.4 = (f32[6]{0:T(128)S(1)}, f32[6]{0:T(128)}, u32[]{:S(2)}) copy-start(f32[6]{0:T(128)} %cour_ref.1) | copy-start | bytes 76
  0.0 0.7 %copy-start.3 = (f32[6]{0:T(128)S(1)}, f32[6]{0:T(128)}, u32[]{:S(2)}) copy-start(f32[6]{0:T(128)} %diff_ref.1) | copy-start | bytes 76
  0.0 0.7 %copy-start.2 = (s32[1,4]{1,0:T(1,128)S(1)}, s32[1,4]{1,0:T(1,128)}, u32[]{:S(2)}) copy-start(s32[1,4]{1,0:T(1,128)} %level_ref.1) | copy-start | bytes 52
  0.7 1.2 %copy-start = (f32[1,2,8,16384]{3,2,1,0:T(8,128)S(1)}, f32[1,2,8,16384]{3,2,1,0:T(8,128)}, u32[]{:S(2)}) copy-start(f32[1,2,8,16384]{3,2,1,0:T(8,128)} %state_ref.1) | copy-start | bytes 3145732
  2.0 1.0 %copy-start.1 = (bf16[256,1024]{1,0:T(8,128)(2,1)S(1)}, bf16[256,1024]{1,0:T(8,128)(2,1)}, u32[]{:S(2)}) copy-start(bf16[256,1024]{1,0:T(8,128)(2,1)} %constant.2.clone.table_hbm) | copy-start | bytes 1572868

commit v2 on v1

--- a/solution.py
+++ b/solution.py
@@ -47,9 +47,10 @@
 
 def constant_table():
     down = kron4(level_matrix(SIDE, -1.0)).T[packed_order()]
-    up = kron4(level_matrix(SIDE, 1.0)).T
+    up = kron4(level_matrix(SIDE, 1.0)).T[:, packed_order()]
     spread = np.kron(interpolation(4), interpolation(8))
-    spread = np.tile(spread, (COARSE // spread.shape[0], 1))
+    spread = spread[packed_order()[:LANES] % spread.shape[0]]
+    spread = np.concatenate([spread, spread], axis=0)
     return np.concatenate([down, up, spread], axis=1).astype(jnp.bfloat16)
 
 
@@ -62,9 +63,9 @@
 
 
 def exact_dot(x, table):
-    high, mid, low = parts_of(x)
-    dot = functools.partial(jnp.dot, preferred_element_type=jnp.float32)
-    return dot(high, table) + (dot(mid, table) + dot(low, table))
+    n = x.shape[0]
+    y = jnp.dot(jnp.concatenate(parts_of(x), axis=0), table, preferred_element_type=jnp.float32)
+    return y[0:n] + (y[n : 2 * n] + y[2 * n : 3 * n])
 
 
 def kernel(
@@ -122,14 +123,12 @@
     tiles = GROUP // LANES
     outer = cells // GROUP
     n3 = 2 * SIDE
-    n2 = outer // n3
 
     def neighbours(g):
-        d2, d3 = g // n3, g % n3
-        starts = []
-        for e2, e3 in ((1, 0), (n2 - 1, 0), (0, 1), (0, n3 - 1)):
-            starts.append(((d2 + e2) % n2 * n3 + (d3 + e3) % n3) * GROUP)
-        return starts
+        base, low = g & ~(n3 - 1), n3 - 1
+        ids = [(g + n3) & (outer - 1), (g - n3) & (outer - 1)]
+        ids += [base | ((g + 1) & low), base | ((g - 1) & low)]
+        return [i * GROUP for i in ids]
 
     def apply_d(ref, r, g):
         here = g * GROUP
@@ -156,7 +155,7 @@
 
     load.wait()
 
-    @pl.loop(0, outer)
+    @pl.loop(0, outer, unroll=2)
     def _(g):
         us, ws = [], []
         for r in range(rows):
@@ -221,7 +220,7 @@
             )
             bulk[-1].start()
 
-    @pl.loop(0, outer)
+    @pl.loop(0, outer, unroll=2)
     def _(g):
         for r in range(rows):
             _, y = apply_d(w, r, g)
@@ -247,14 +246,21 @@
     def placement(flat):
         target = jnp.zeros_like(flat)
         for p in range(4):
-            target = target + flat // SIDE ** (3 - p) % SIDE * scale[p]
+            target = target + ((flat >> LOW * (3 - p)) & (SIDE - 1)) * scale[p]
         return target
 
     row_id = lax.broadcasted_iota(jnp.int32, (COARSE, COARSE), 0)
     col_id = lax.broadcasted_iota(jnp.int32, (COARSE, COARSE), 1)
+    col_line = lax.broadcasted_iota(jnp.int32, (1, COARSE), 1)
+    row_line = lax.broadcasted_iota(jnp.int32, (COARSE, LANES), 0)
     one = lambda hit: jnp.where(hit, 1.0, 0.0).astype(jnp.bfloat16)
-    forward = one(row_id == placement(col_id))
-    backward = one(col_id == placement(row_id))
+    forward = one(row_id == placement(col_line))
+    row_target = placement(row_line)
+    backward = one(col_id == jnp.concatenate([row_target] * (COARSE // LANES), axis=1))
+    load_table.wait()
+    dot = functools.partial(jnp.dot, preferred_element_type=jnp.float32)
+    forward = dot(table[:, 0:COARSE], forward).astype(jnp.bfloat16)
+    backward = dot(backward, table[:, COARSE : 2 * COARSE]).astype(jnp.bfloat16)
 
     pieces = [jnp.concatenate(pack(acc, r), axis=1) for r in range(rows)]
     for s in range(2):
@@ -264,9 +270,7 @@
     pieces[rows - 1] += c_in[1, 1]
     pieces[rows - 2] += a[0] * a[0] * c_in[1, 0]
     points = jnp.concatenate(pieces, axis=0)
-    load_table.wait()
-    surplus = exact_dot(points, table[:, 0:COARSE])
-    weighted = weight_ref[0].astype(jnp.float32) * exact_dot(surplus, forward)
+    weighted = weight_ref[0].astype(jnp.float32) * exact_dot(points, forward)
     g_out[...] = weighted
     shares = []
     for k, peer in enumerate(peers):
@@ -282,24 +286,27 @@
     for k in range(len(peers)):
         shares[k].wait_recv()
         combined = combined + g_in[k]
-    change = exact_dot(combined, backward) - surplus
-    change = exact_dot(change, table[:, COARSE : 2 * COARSE])
-
-    per_group = 16
-    for g in range(COARSE // per_group):
-        half, place = g * per_group // LANES, g % (LANES // per_group)
-        x = change[:, half * LANES : (half + 1) * LANES]
-        block = lax.broadcasted_iota(jnp.int32, x.shape, 1) // per_group
-        x = jnp.where(block == place, x, 0.0)
-        z[g] = exact_dot(x, table[0:LANES, 2 * COARSE :])
+    change = exact_dot(combined, backward) - points
+
+    place = lax.broadcasted_iota(jnp.int32, (rows * second, LANES), 1)
+    place = (place >> 5) * 2 + ((place >> 2) & 1)
+    left = []
+    for g in range(SIDE * SIDE):
+        half = g // 8
+        x = jnp.where(place == g % 8, change[:, half * LANES : (half + 1) * LANES], 0.0)
+        high = x.astype(jnp.bfloat16)
+        mid = (x - high.astype(jnp.float32)).astype(jnp.bfloat16)
+        left.append(jnp.concatenate([high, mid], axis=1))
+    fine = dot(jnp.concatenate(left, axis=0), table[:, 2 * COARSE :])
+    for g in range(SIDE * SIDE):
+        z[g] = fine[g * rows * second : (g + 1) * rows * second]
 
     for s in range(2):
         raw[s].wait_recv()
 
     @pl.loop(0, outer // 2)
     def _(i):
-        d2, c3 = i // SIDE, i % SIDE
-        after = d2 * SIDE + (c3 + 1) % SIDE
+        after = (i & ~(SIDE - 1)) | ((i + 1) & (SIDE - 1))
         for r in range(rows):
             for t in range(tiles):
                 cut = (pl.ds(r * second, second), slice(t * LANES, (t + 1) * LANES))
@@ -317,7 +324,7 @@
         for s in range(2):
             bulk[2 * c + s].wait_recv()
 
-        @pl.loop(0, width // GROUP)
+        @pl.loop(0, width // GROUP, unroll=2)
         def _(i):
             for t in range(tiles):
                 here = spot(c * (width // GROUP) + i, t)
@@ -372,7 +379,7 @@
             dma((chunks,)),
         ],
         compiler_params=pltpu.CompilerParams(
-            collective_id=0, has_side_effects=True, vmem_limit_bytes=40 * 2**20
+            collective_id=0, has_side_effects=True, vmem_limit_bytes=62 * 2**20
         ),
     )(level_vectors, combine_weights, diffusion, courant, state_field, table)
 

time: 34.8 us -> 34.8 us (level)
  Pallas kernels: 30.7 us -> 31.7 us
  local copies, waits for them, and re-layouts: 3.24 us -> 2.26 us
    pallas_call x1, Pallas kernels: 30.7 us -> 31.7 us  [local(): pl.pallas_call(functools.partial(kernel, grids, doms, chunks), out_shape=...]
    unnamed x11 -> x1, local copies, waits for them, and re-layouts: 3.24 us -> 2.26 us
where the time goes in v2:
time: 34.8 us; the launch traced here: 34.6 us
  Pallas kernels  31.7 us (91%)
  local copies, waits for them, and re-layouts  2.26 us (6%)
  between operations  0.66 us (2%)
    pallas_call x1, Pallas kernels, local(): pl.pallas_call(functools.partial(kernel, grids, doms, chunks), out_shape=...  31.7 us
    unnamed x1, local copies, waits for them, and re-layouts  2.26 us

profile of v2, /device:TPU:0, one launch (start us, length us, event | category | flops | bytes accessed | tf_op | source)
XLA Modules:
  0.0 34.6 jit_solution(17963248340677354228)
XLA Ops:
  0.7 31.7 %shard_map.64 = f32[1,2,8,16384]{3,2,1,0:T(8,128)} custom-call(s32[1,4]{1,0:T(1,128)} %level_ref.1, s32[1]{0:T(128)S(6)} %copy.8.weight_ref, f32[6]{0:T(128)} %diff_ref.1, f32[6]{0:T(128)} %cour_ref.1, f32[1,2,8,16384]{3,2,1,0:T(8,128)} %state_ref.1, bf16[256,1024]{1,0:T(8,128)(2,1)} %constant.2.clone.table_hbm), custom_call_target="tpu_custom_call" | custom-call | tf_op jit(solution)/shard_map/pallas_call | solution.py:352
  32.3 2.3 %copy.9 = f32[1,2,8,16384]{3,2,1,0:T(8,128)} copy(f32[1,2,8,16384]{3,2,1,0:T(8,128)} %shard_map.64) | data formatting | bytes 2097152

commit v3 on v2

--- a/solution.py
+++ b/solution.py
@@ -71,8 +71,8 @@
 def kernel(
     grids, doms, chunks,
     level_ref, weight_ref, diff_ref, cour_ref, state_ref, table_hbm,
-    out_ref,
-    u, w, acc, near, far, mine, table, c_out, c_in, g_out, g_in, z,
+    out_ref, far,
+    u, w, acc, near, mine, table, c_out, c_in, g_out, g_in, z,
     in_sem, raw_s, raw_r, far_s, far_r, cs, cr, gs, gr, out_sem,
 ):
     rows, second, cells = u.shape
@@ -319,25 +319,13 @@
                         x += a[0] * a[0] * near[1, :, spot(2 * i + h, t)]
                     acc[r, :, spot(2 * i + h, t)] += x
 
-    saves = []
-    for c in range(chunks):
-        for s in range(2):
-            bulk[2 * c + s].wait_recv()
-
-        @pl.loop(0, width // GROUP, unroll=2)
-        def _(i):
-            for t in range(tiles):
-                here = spot(c * (width // GROUP) + i, t)
-                acc[0, :, here] += far[0, :, here]
-                acc[rows - 1, :, here] += far[1, :, here]
-
-        cut = (slice(None), slice(None), pl.ds(c * width, width))
-        saves.append(pltpu.make_async_copy(acc.at[cut], out_ref.at[(0,) + cut], out_sem.at[c]))
-        saves[-1].start()
+    save = pltpu.make_async_copy(acc, out_ref, out_sem.at[0])
+    save.start()
+    for copy in bulk:
+        copy.wait_recv()
     for copy in raw + coarse + bulk + shares:
         copy.wait_send()
-    for copy in saves:
-        copy.wait()
+    save.wait()
 
 
 def local(grids, doms, state_field, level_vectors, combine_weights, diffusion, courant):
@@ -349,16 +337,18 @@
     smem = pl.BlockSpec(memory_space=pltpu.SMEM)
     anywhere = pl.BlockSpec(memory_space=pl.ANY)
     others = max(grids - 1, 1)
-    return pl.pallas_call(
+    own, far = pl.pallas_call(
         functools.partial(kernel, grids, doms, chunks),
-        out_shape=jax.ShapeDtypeStruct(state_field.shape, f32),
-        in_specs=[smem] * 4 + [anywhere] * 2,
-        out_specs=anywhere,
+        out_shape=[
+            jax.ShapeDtypeStruct((rows, second, cells), f32),
+            jax.ShapeDtypeStruct((2, second, cells), f32),
+        ],
+        in_specs=[smem] * 4 + [pl.BlockSpec(memory_space=pltpu.HBM)] * 2,
+        out_specs=[anywhere] * 2,
         scratch_shapes=[
             pltpu.VMEM((rows, second, cells), f32),
             pltpu.VMEM((rows, second, cells), f32),
             pltpu.VMEM((rows, second, cells), f32),
-            pltpu.VMEM((2, second, cells), f32),
             pltpu.VMEM((2, second, cells), f32),
             pltpu.VMEM((2, second, cells), f32),
             pltpu.VMEM(table.shape, jnp.bfloat16),
@@ -376,12 +366,16 @@
             dma((2,)),
             dma((others,)),
             dma((others,)),
-            dma((chunks,)),
+            dma((1,)),
         ],
         compiler_params=pltpu.CompilerParams(
-            collective_id=0, has_side_effects=True, vmem_limit_bytes=62 * 2**20
+            collective_id=0, has_side_effects=True, vmem_limit_bytes=40 * 2**20
         ),
     )(level_vectors, combine_weights, diffusion, courant, state_field, table)
+    if rows == 2:
+        return (own + far)[None]
+    parts = [own[:1] + far[:1], own[1:-1], own[-1:] + far[1:]]
+    return jnp.concatenate(parts, axis=0)[None]
 
 
 def solution(mesh):

time: 34.8 us -> 34.8 us (level)
  Pallas kernels: 31.7 us -> 30.5 us
  other arithmetic: 0 us -> 1.08 us
    pallas_call x1, Pallas kernels: 31.7 us -> 30.5 us  [local(): pl.pallas_call(functools.partial(kernel, grids, doms, chunks), out_shape=...]
    broadcast_in_dim x0 -> x1, other arithmetic: none -> 1.08 us  [local(): return (own + far)[None]]
    unnamed x1 -> x10, local copies, waits for them, and re-layouts: 2.26 us -> 2.27 us
where the time goes in v3:
time: 34.8 us; the launch traced here: 34.6 us
  Pallas kernels  30.5 us (88%)
  local copies, waits for them, and re-layouts  2.27 us (7%)
  other arithmetic  1.08 us (3%)
  between operations  0.74 us (2%)
    pallas_call x1, Pallas kernels, local(): pl.pallas_call(functools.partial(kernel, grids, doms, chunks), out_shape=...  30.5 us
    unnamed x10, local copies, waits for them, and re-layouts  2.27 us
    broadcast_in_dim x1, other arithmetic, local(): return (own + far)[None]  1.08 us

profile of v3, /device:TPU:0, one launch (start us, length us, event | category | flops | bytes accessed | tf_op | source)
XLA Modules:
  0.0 34.6 jit_solution(8093154705808953502)
XLA Ops:
  0.0 0.0 copy-start.4
  0.0 0.0 copy-start.3
  0.0 0.0 copy-start.2
  0.7 0.0 copy-done.4
  0.7 0.0 copy-done.3
  0.7 0.0 copy-done.2
  0.7 0.0 copy-start
  0.7 1.2 %copy-done = f32[1,2,8,16384]{3,2,1,0:T(8,128)S(1)} copy-done((f32[1,2,8,16384]{3,2,1,0:T(8,128)S(1)}, f32[1,2,8,16384]{3,2,1,0:T(8,128)}, u32[]{:S(2)}) %copy-start) | copy-done | bytes 1048600
  2.0 0.0 copy-start.1
  2.0 1.0 %copy-done.1 = bf16[256,1024]{1,0:T(8,128)(2,1)S(1)} copy-done((bf16[256,1024]{1,0:T(8,128)(2,1)S(1)}, bf16[256,1024]{1,0:T(8,128)(2,1)}, u32[]{:S(2)}) %copy-start.1) | copy-done | bytes 524312
  3.0 30.5 %shard_map.64 = (f32[2,8,16384]{2,1,0:T(8,128)S(1)}, f32[2,8,16384]{2,1,0:T(8,128)S(1)}) custom-call(s32[1,4]{1,0:T(1,128)S(1)} %copy-done.2, s32[1]{0:T(128)S(6)} %copy.7.weight_ref, f32[6]{0:T(128)S(1)} %copy-done.3, f32[6]{0:T(128)S(1)} %copy-done.4, f32[1,2,8,16384]{3,2,1,0:T(8,128)S(1)} %copy-done, bf16[256,1024]{1,0:T(8,128)(2,1)S(1)} %copy-done.1), custom_call_target="tpu_custom_call" | custom-call | tf_op jit(solution)/shard_map/pallas_call | solution.py:340
  33.5 1.1 %add_bitcast_fusion = f32[1,2,8,16384]{3,2,1,0:T(8,128)} fusion(f32[2,8,16384]{2,1,0:T(8,128)S(1)} %get-tuple-element.7, f32[2,8,16384]{2,1,0:T(8,128)S(1)} %get-tuple-element.8), kind=kLoop, calls=%fused_computation | loop fusion | flops 262144 | bytes 3145728 | tf_op jit(solution)/shard_map/broadcast_in_dim | solution.py:376
Async XLA Ops:
  0.0 0.7 %copy-start.4 = (f32[6]{0:T(128)S(1)}, f32[6]{0:T(128)}, u32[]{:S(2)}) copy-start(f32[6]{0:T(128)} %cour_ref.1) | copy-start | bytes 76
  0.0 0.7 %copy-start.3 = (f32[6]{0:T(128)S(1)}, f32[6]{0:T(128)}, u32[]{:S(2)}) copy-start(f32[6]{0:T(128)} %diff_ref.1) | copy-start | bytes 76
  0.0 0.7 %copy-start.2 = (s32[1,4]{1,0:T(1,128)S(1)}, s32[1,4]{1,0:T(1,128)}, u32[]{:S(2)}) copy-start(s32[1,4]{1,0:T(1,128)} %level_ref.1) | copy-start | bytes 52
  0.7 1.2 %copy-start = (f32[1,2,8,16384]{3,2,1,0:T(8,128)S(1)}, f32[1,2,8,16384]{3,2,1,0:T(8,128)}, u32[]{:S(2)}) copy-start(f32[1,2,8,16384]{3,2,1,0:T(8,128)} %state_ref.1) | copy-start | bytes 3145732
  2.0 1.0 %copy-start.1 = (bf16[256,1024]{1,0:T(8,128)(2,1)S(1)}, bf16[256,1024]{1,0:T(8,128)(2,1)}, u32[]{:S(2)}) copy-start(bf16[256,1024]{1,0:T(8,128)(2,1)} %constant.2.clone.table_hbm) | copy-start | bytes 1572868

commit v4 on v3

--- a/solution.py
+++ b/solution.py
@@ -369,7 +369,7 @@
             dma((1,)),
         ],
         compiler_params=pltpu.CompilerParams(
-            collective_id=0, has_side_effects=True, vmem_limit_bytes=40 * 2**20
+            collective_id=0, has_side_effects=True, vmem_limit_bytes=62 * 2**20
         ),
     )(level_vectors, combine_weights, diffusion, courant, state_field, table)
     if rows == 2:

time: 34.8 us -> 34.4 us (0.989)
  local copies, waits for them, and re-layouts: 2.27 us -> 0 us
  other arithmetic: 1.08 us -> 2.62 us
  Pallas kernels: 30.5 us -> 30.9 us
    unnamed x10 -> x0, local copies, waits for them, and re-layouts: 2.27 us -> none
    broadcast_in_dim x1, other arithmetic: 1.08 us -> 2.62 us  [local(): return (own + far)[None]]
    pallas_call x1, Pallas kernels: 30.5 us -> 30.9 us  [local(): pl.pallas_call(functools.partial(kernel, grids, doms, chunks), out_shape=...]
where the time goes in v4:
time: 34.4 us; the launch traced here: 34.2 us
  Pallas kernels  30.9 us (90%)
  other arithmetic  2.62 us (8%)
  between operations  0.66 us (2%)
    pallas_call x1, Pallas kernels, local(): pl.pallas_call(functools.partial(kernel, grids, doms, chunks), out_shape=...  30.9 us
    broadcast_in_dim x1, other arithmetic, local(): return (own + far)[None]  2.62 us

profile of v4, /device:TPU:0, one launch (start us, length us, event | category | flops | bytes accessed | tf_op | source)
XLA Modules:
  0.0 34.2 jit_solution(6001350538360470606)
XLA Ops:
  0.7 30.9 %shard_map.64 = (f32[2,8,16384]{2,1,0:T(8,128)}, f32[2,8,16384]{2,1,0:T(8,128)}) custom-call(s32[1,4]{1,0:T(1,128)} %level_ref.1, s32[1]{0:T(128)S(6)} %copy.7.weight_ref, f32[6]{0:T(128)} %diff_ref.1, f32[6]{0:T(128)} %cour_ref.1, f32[1,2,8,16384]{3,2,1,0:T(8,128)} %state_ref.1, bf16[256,1024]{1,0:T(8,128)(2,1)} %constant.2.clone.table_hbm), custom_call_target="tpu_custom_call" | custom-call | tf_op jit(solution)/shard_map/pallas_call | solution.py:340
  31.6 2.6 %add_bitcast_fusion = f32[1,2,8,16384]{3,2,1,0:T(8,128)} fusion(f32[2,8,16384]{2,1,0:T(8,128)} %get-tuple-element.7, f32[2,8,16384]{2,1,0:T(8,128)} %get-tuple-element.8), kind=kLoop, calls=%fused_computation | loop fusion | flops 262144 | bytes 3145728 | tf_op jit(solution)/shard_map/broadcast_in_dim | solution.py:376

commit v5 on v3

--- a/solution.py
+++ b/solution.py
@@ -331,7 +331,8 @@
 def local(grids, doms, state_field, level_vectors, combine_weights, diffusion, courant):
     _, rows, second, cells = state_field.shape
     chunks = 4
-    table = jnp.asarray(constant_table())
+    table = pltpu.with_memory_space_constraint(jnp.asarray(constant_table()), pltpu.HBM)
+    state_in = pltpu.with_memory_space_constraint(state_field, pltpu.HBM)
     f32 = jnp.float32
     dma = pltpu.SemaphoreType.DMA
     smem = pl.BlockSpec(memory_space=pltpu.SMEM)
@@ -371,7 +372,7 @@
         compiler_params=pltpu.CompilerParams(
             collective_id=0, has_side_effects=True, vmem_limit_bytes=40 * 2**20
         ),
-    )(level_vectors, combine_weights, diffusion, courant, state_field, table)
+    )(level_vectors, combine_weights, diffusion, courant, state_in, table)
     if rows == 2:
         return (own + far)[None]
     parts = [own[:1] + far[:1], own[1:-1], own[-1:] + far[1:]]

time: 34.8 us -> 32.7 us (0.940)
  local copies, waits for them, and re-layouts: 2.27 us -> 0.01 us
    unnamed x10 -> x6, local copies, waits for them, and re-layouts: 2.27 us -> 0.01 us
where the time goes in v5:
time: 32.7 us; the launch traced here: 32.5 us
  Pallas kernels  30.7 us (94%)
  other arithmetic  1.08 us (3%)
  between operations  0.73 us (2%)
    pallas_call x1, Pallas kernels, local(): pl.pallas_call(functools.partial(kernel, grids, doms, chunks), out_shape=...  30.7 us
    broadcast_in_dim x1, other arithmetic, local(): return (own + far)[None]  1.08 us

profile of v5, /device:TPU:0, one launch (start us, length us, event | category | flops | bytes accessed | tf_op | source)
XLA Modules:
  0.0 32.5 jit_solution(6141903087750604956)
XLA Ops:
  0.0 0.0 copy-start.2
  0.0 0.0 copy-start.1
  0.0 0.0 copy-start
  0.7 0.0 copy-done.2
  0.7 0.0 copy-done.1
  0.7 0.0 copy-done
  0.7 30.7 %shard_map.64 = (f32[2,8,16384]{2,1,0:T(8,128)S(1)}, f32[2,8,16384]{2,1,0:T(8,128)S(1)}) custom-call(s32[1,4]{1,0:T(1,128)S(1)} %copy-done, s32[1]{0:T(128)S(6)} %copy.7.weight_ref, f32[6]{0:T(128)S(1)} %copy-done.1, f32[6]{0:T(128)S(1)} %copy-done.2, f32[1,2,8,16384]{3,2,1,0:T(8,128)} %state_ref.1, bf16[256,1024]{1,0:T(8,128)(2,1)} %constant.2.clone.table_hbm), custom_call_target="tpu_custom_call" | custom-call | tf_op jit(solution)/shard_map/pallas_call | solution.py:341
  31.5 1.1 %add_bitcast_fusion = f32[1,2,8,16384]{3,2,1,0:T(8,128)} fusion(f32[2,8,16384]{2,1,0:T(8,128)S(1)} %get-tuple-element.7, f32[2,8,16384]{2,1,0:T(8,128)S(1)} %get-tuple-element.8), kind=kLoop, calls=%fused_computation | loop fusion | flops 262144 | bytes 3145728 | tf_op jit(solution)/shard_map/broadcast_in_dim | solution.py:377
Async XLA Ops:
  0.0 0.7 %copy-start.2 = (f32[6]{0:T(128)S(1)}, f32[6]{0:T(128)}, u32[]{:S(2)}) copy-start(f32[6]{0:T(128)} %cour_ref.1) | copy-start | bytes 76
  0.0 0.7 %copy-start.1 = (f32[6]{0:T(128)S(1)}, f32[6]{0:T(128)}, u32[]{:S(2)}) copy-start(f32[6]{0:T(128)} %diff_ref.1) | copy-start | bytes 76
  0.0 0.7 %copy-start = (s32[1,4]{1,0:T(1,128)S(1)}, s32[1,4]{1,0:T(1,128)}, u32[]{:S(2)}) copy-start(s32[1,4]{1,0:T(1,128)} %level_ref.1) | copy-start | bytes 52

commit v6 on v5

--- a/solution.py
+++ b/solution.py
@@ -70,9 +70,10 @@
 
 def kernel(
     grids, doms, chunks,
-    level_ref, weight_ref, diff_ref, cour_ref, state_ref, table_hbm,
+    weight_ref, level_hbm, diff_hbm, cour_hbm, state_ref, table_hbm,
     out_ref, far,
     u, w, acc, near, mine, table, c_out, c_in, g_out, g_in, z,
+    level_ref, diff_ref, cour_ref,
     in_sem, raw_s, raw_r, far_s, far_r, cs, cr, gs, gr, out_sem,
 ):
     rows, second, cells = u.shape
@@ -89,6 +90,16 @@
     load.start()
     load_table = pltpu.make_async_copy(table_hbm, table, in_sem.at[1])
     load_table.start()
+    smalls = []
+    for k, (src, dst) in enumerate(
+        (
+            (level_hbm, level_ref),
+            (diff_hbm, diff_ref),
+            (cour_hbm, cour_ref),
+        )
+    ):
+        smalls.append(pltpu.make_async_copy(src, dst, in_sem.at[2 + k]))
+        smalls[-1].start()
     pl.semaphore_wait(barrier, 2 + len(peers))
 
     targets = ((gi, above), (gi, below))
@@ -103,6 +114,8 @@
         )
         raw[-1].start()
 
+    for copy in smalls:
+        copy.wait()
     kappa, sigma = [diff_ref[0], diff_ref[1]], [cour_ref[0], cour_ref[1]]
     for j in range(4):
         k_sum, s_sum = jnp.float32(0.0), jnp.float32(0.0)
@@ -335,6 +348,8 @@
     state_in = pltpu.with_memory_space_constraint(state_field, pltpu.HBM)
     f32 = jnp.float32
     dma = pltpu.SemaphoreType.DMA
+    hbm = lambda x: pltpu.with_memory_space_constraint(x, pltpu.HBM)
+    small = [hbm(x) for x in (level_vectors, diffusion, courant)]
     smem = pl.BlockSpec(memory_space=pltpu.SMEM)
     anywhere = pl.BlockSpec(memory_space=pl.ANY)
     others = max(grids - 1, 1)
@@ -344,7 +359,7 @@
             jax.ShapeDtypeStruct((rows, second, cells), f32),
             jax.ShapeDtypeStruct((2, second, cells), f32),
         ],
-        in_specs=[smem] * 4 + [pl.BlockSpec(memory_space=pltpu.HBM)] * 2,
+        in_specs=[smem] + [pl.BlockSpec(memory_space=pltpu.HBM)] * 5,
         out_specs=[anywhere] * 2,
         scratch_shapes=[
             pltpu.VMEM((rows, second, cells), f32),
@@ -358,7 +373,10 @@
             pltpu.VMEM((rows * second, COARSE), f32),
             pltpu.VMEM((others, rows * second, COARSE), f32),
             pltpu.VMEM((SIDE * SIDE, rows * second, GROUP), f32),
-            dma((2,)),
+            pltpu.SMEM(level_vectors.shape, jnp.int32),
+            pltpu.SMEM(diffusion.shape, f32),
+            pltpu.SMEM(courant.shape, f32),
+            dma((5,)),
             dma((2,)),
             dma((2,)),
             dma((2, chunks)),
@@ -372,7 +390,7 @@
         compiler_params=pltpu.CompilerParams(
             collective_id=0, has_side_effects=True, vmem_limit_bytes=40 * 2**20
         ),
-    )(level_vectors, combine_weights, diffusion, courant, state_in, table)
+    )(combine_weights, *small, state_in, table)
     if rows == 2:
         return (own + far)[None]
     parts = [own[:1] + far[:1], own[1:-1], own[-1:] + far[1:]]

time: 32.7 us -> 32.1 us (0.982)
  Pallas kernels: 30.7 us -> 30.2 us
    pallas_call x1, Pallas kernels: 30.7 us -> 30.2 us  [local(): pl.pallas_call(functools.partial(kernel, grids, doms, chunks), out_shape=...]
where the time goes in v6:
time: 32.1 us; the launch traced here: 31.9 us
  Pallas kernels  30.2 us (94%)
  other arithmetic  1.08 us (3%)
  between operations  0.66 us (2%)
    pallas_call x1, Pallas kernels, local(): pl.pallas_call(functools.partial(kernel, grids, doms, chunks), out_shape=...  30.2 us
    broadcast_in_dim x1, other arithmetic, local(): return (own + far)[None]  1.08 us

profile of v6, /device:TPU:0, one launch (start us, length us, event | category | flops | bytes accessed | tf_op | source)
XLA Modules:
  0.0 31.9 jit_solution(16067206498112352395)
XLA Ops:
  0.7 30.2 %shard_map.64 = (f32[2,8,16384]{2,1,0:T(8,128)S(1)}, f32[2,8,16384]{2,1,0:T(8,128)S(1)}) custom-call(s32[1]{0:T(128)S(6)} %copy.7.weight_ref, s32[1,4]{1,0:T(1,128)} %level_hbm.1, f32[6]{0:T(128)} %diff_hbm.1, f32[6]{0:T(128)} %cour_hbm.1, f32[1,2,8,16384]{3,2,1,0:T(8,128)} %state_ref.1, bf16[256,1024]{1,0:T(8,128)(2,1)} %constant.2.clone.table_hbm), custom_call_target="tpu_custom_call" | custom-call | tf_op jit(solution)/shard_map/pallas_call | solution.py:356
  30.8 1.1 %add_bitcast_fusion = f32[1,2,8,16384]{3,2,1,0:T(8,128)} fusion(f32[2,8,16384]{2,1,0:T(8,128)S(1)} %get-tuple-element.7, f32[2,8,16384]{2,1,0:T(8,128)S(1)} %get-tuple-element.8), kind=kLoop, calls=%fused_computation | loop fusion | flops 262144 | bytes 3145728 | tf_op jit(solution)/shard_map/broadcast_in_dim | solution.py:395
